TPU v7x, 256 devices: a whole 4x4x8 slice. The times are simulated.
256 devices in a mesh: section: 32 (over z, x), dp: 8 (over y, core).
Axes of the slice: x: 4, y: 4, z: 8, core: 2. Of those that a mesh axis runs over, the one named last changes fastest.
Arguments:
- inputs: bfloat16 [1024, 4096], P('dp'), may hold values from -6 to 6
- gains: float32 [32, 4096], P('section'), may hold values from 0.1 to 1.9
- w_query: bfloat16 [32, 4096, 2048], P('section', 'dp'), may hold values from -0.09375 to 0.09375
- w_key: bfloat16 [32, 4096, 512], P('section', 'dp'), may hold values from -0.09375 to 0.09375
- w_value: bfloat16 [32, 4096, 512], P('section', 'dp'), may hold values from -0.09375 to 0.09375
- w_out: bfloat16 [32, 2048, 4096], P('section', 'dp'), may hold values from -0.125 to 0.125
Outputs:
- section_outputs: bfloat16 [32, 1024, 4096], P('section', 'dp')
All inputs are finite; a program needn't handle non-finite values.
Results may differ from a plain program's by a relative error of at most 0.035.
Values may be sent and summed in bfloat16 or wider, within the bound.
A program may use at most 128 MiB of HBM per device.

v0:
```python
import jax
import jax.numpy as jnp
from jax import lax
from jax.sharding import PartitionSpec as P

HEADS = 16
KV = 4
HDIM = 128
BLOCKS = 4


def passed_along(value, axis, steps):
    count = lax.axis_size(axis)
    initial, last = (max(0, -steps), min(count, count - steps))
    return lax.ppermute(value, axis, [(source, source + steps) for source in range(initial, last)])


def on_device(inputs, gains, w_query, w_key, w_value, w_out):
    full_query, full_key, full_value, full_out = (
        lax.all_gather(w_query, "dp", axis=1, tiled=True),
        lax.all_gather(w_key, "dp", axis=1, tiled=True),
        lax.all_gather(w_value, "dp", axis=1, tiled=True),
        lax.all_gather(w_out, "dp", axis=1, tiled=True),
    )
    weight_q = full_query[0]
    weight_k = full_key[0]
    weight_v = full_value[0]
    weight_o = full_out[0]
    gain = gains[0]
    section_pos = lax.axis_index("section")
    sections = lax.axis_size("section")
    seq_rows = inputs.shape[0]
    width = inputs.shape[1]
    kv_width = weight_k.shape[1]
    groups = HEADS // KV
    pieces = BLOCKS
    rows = seq_rows // pieces
    scale = 1.0 / HDIM**0.5
    key_pos = jnp.arange(seq_rows, dtype=jnp.int32)

    def attend(normed, keys, values, index):
        query = jnp.dot(normed, weight_q, preferred_element_type=jnp.float32).astype(jnp.bfloat16)
        query_r = query.reshape(rows, KV, groups, HDIM)
        keys_r = keys.reshape(seq_rows, KV, HDIM)
        values_r = values.reshape(seq_rows, KV, HDIM)
        scores = (
            jnp.einsum("pkgd,skd->kgps", query_r, keys_r, preferred_element_type=jnp.float32)
            * scale
        )
        query_pos = index * rows + jnp.arange(rows, dtype=jnp.int32)
        allowed = key_pos[None, :] <= query_pos[:, None]
        scores = jnp.where(allowed, scores, -1e30)
        peak = jnp.max(scores, axis=-1, keepdims=True)
        expo = jnp.exp(scores - peak)
        probs = (expo / jnp.sum(expo, axis=-1, keepdims=True)).astype(jnp.bfloat16)
        attended = jnp.einsum(
            "kgps,skd->pkgd", probs, values_r, preferred_element_type=jnp.float32
        ).astype(jnp.bfloat16)
        return attended.reshape(rows, HEADS * HDIM)

    def run(operands):
        piece, index, store, outputs = operands
        xf = piece.astype(jnp.float32)
        normed = (xf * lax.rsqrt(jnp.mean(xf * xf, axis=-1, keepdims=True) + 1e-05) * gain).astype(
            jnp.bfloat16
        )
        key_store, value_store = store
        new_keys = jnp.dot(normed, weight_k, preferred_element_type=jnp.float32).astype(
            jnp.bfloat16
        )
        new_values = jnp.dot(normed, weight_v, preferred_element_type=jnp.float32).astype(
            jnp.bfloat16
        )
        key_store = lax.dynamic_update_slice_in_dim(key_store, new_keys, index * rows, 0)
        value_store = lax.dynamic_update_slice_in_dim(value_store, new_values, index * rows, 0)
        keys, values = (key_store, value_store)
        store = (key_store, value_store)
        attended = attend(normed, keys, values, index)
        result = (xf + jnp.dot(attended, weight_o, preferred_element_type=jnp.float32)).astype(
            jnp.bfloat16
        )
        outputs = lax.dynamic_update_slice_in_dim(outputs, result, index * rows, 0)
        return (result, store, outputs)

    def skip(operands):
        piece, index, store, outputs = operands
        return (jnp.zeros_like(piece), store, outputs)

    def tick(step, carry):
        incoming, store, outputs = carry
        index = step - section_pos
        active = jnp.logical_and(index >= 0, index < pieces)
        safe = jnp.clip(index, 0, pieces - 1)
        first = lax.dynamic_slice_in_dim(inputs, safe * rows, rows, 0)
        piece = jnp.where(section_pos == 0, first, incoming)
        result, store, outputs = lax.cond(active, run, skip, (piece, safe, store, outputs))
        incoming = passed_along(result, "section", 1)
        return (incoming, store, outputs)

    store = (
        jnp.zeros((seq_rows, kv_width), jnp.bfloat16),
        jnp.zeros((seq_rows, kv_width), jnp.bfloat16),
    )
    start = (
        jnp.zeros((rows, width), jnp.bfloat16),
        store,
        jnp.zeros((seq_rows, width), jnp.bfloat16),
    )
    final_in, final_store, outputs = lax.fori_loop(0, pieces + sections - 1, tick, start)
    return outputs[None]


def solution(mesh):
    in_specs = (
        P("dp", None),
        P("section", None),
        P("section", "dp", None),
        P("section", "dp", None),
        P("section", "dp", None),
        P("section", "dp", None),
    )
    out_specs = P("section", "dp", None)
    return jax.shard_map(
        on_device, mesh=mesh, in_specs=in_specs, out_specs=out_specs, check_vma=False
    )
```

profile of v0, /device:TPU:230, one launch (start us, length us, event | category | flops | bytes accessed | tf_op | source)
XLA Modules:
  0.0 1382.2 jit_solution(8641679016488688054)
XLA Ops:
  9.3 35.0 %all-gather.7.cloned.1.call-done = bf16[1,4096,512]{2,1,0:T(8,128)(2,1)} async-done(((bf16[1,512,512]{2,1,0:T(8,128)(2,1)}), bf16[1,4096,512]{2,1,0:T(8,128)(2,1)}) %all-gather.7.cloned.1.call-update) | async-done | bytes 4194320 | tf_op jit(solution)/shard_map/all_gather | solution.py:21
  44.3 36.5 %all-gather.5.cloned.1.call-done = bf16[1,4096,512]{2,1,0:T(8,128)(2,1)} async-done(((bf16[1,512,512]{2,1,0:T(8,128)(2,1)}), bf16[1,4096,512]{2,1,0:T(8,128)(2,1)}) %all-gather.5.cloned.1.call-update) | async-done | bytes 4194320 | tf_op jit(solution)/shard_map/all_gather | solution.py:22
  80.8 89.4 %all-gather.9.cloned.1.call-done = bf16[1,4096,2048]{2,1,0:T(8,128)(2,1)} async-done(((bf16[1,512,2048]{2,1,0:T(8,128)(2,1)}), bf16[1,4096,2048]{2,1,0:T(8,128)(2,1)}) %all-gather.9.cloned.1.call-update) | async-done | bytes 16777232 | tf_op jit(solution)/shard_map/all_gather | solution.py:20
  170.2 89.9 %all-gather.11.cloned.1.call-done = bf16[1,2048,4096]{2,1,0:T(8,128)(2,1)} async-done(((bf16[1,256,4096]{2,1,0:T(8,128)(2,1)}), bf16[1,2048,4096]{2,1,0:T(8,128)(2,1)}) %all-gather.11.cloned.1.call-update) | async-done | bytes 16777232 | tf_op jit(solution)/shard_map/all_gather | solution.py:23
  260.3 1114.4 %while.21 = (s32[]{:T(128)}, bf16[32,4096]{1,0:T(8,128)(2,1)S(1)}, bf16[128,512]{1,0:T(8,128)(2,1)S(1)}, bf16[128,512]{1,0:T(8,128)(2,1)S(1)}, bf16[128,4096]{1,...) while((s32[]{:T(128)}, bf16[32,4096]{1,0:T(8,128)(2,1)S(1)}, ...), condition=%wide.region_6.7_spmd.clone, body=%wide.region_0.6_spmd.clone.sunk | while | flops 1378849536 | bytes 81919248 | solution.py:109
  339.0 10.9 collective-permute-done
  351.3 12.7 collective-permute-done
  365.4 11.3 collective-permute-done
  378.0 10.0 collective-permute-done
  429.2 9.8 collective-permute-done
  440.4 11.3 collective-permute-done
  453.1 12.5 collective-permute-done
  466.9 11.1 collective-permute-done
  479.4 10.4 collective-permute-done
  531.0 9.8 collective-permute-done
  542.2 11.3 collective-permute-done
  583.1 652.6 %collective-permute-done = bf16[32,4096]{1,0:T(8,128)(2,1)S(1)} collective-permute-done((bf16[32,4096]{1,0:T(8,128)(2,1)S(1)}, bf16[32,4096]{1,0:T(8,128)(2,1)S(1)}, u32[]{:S(2)}, u32[]{:S(2)}) %collective-permute-start) | collective-permute-done | bytes 262176 | tf_op jit(solution)/shard_map/while/body/eval_jaxpr/ppermute | solution.py:15
  1235.7 23.8 %conditional.3 = (bf16[32,4096]{1,0:T(8,128)(2,1)S(1)}, bf16[128,512]{1,0:T(8,128)(2,1)S(1)}, bf16[128,512]{1,0:T(8,128)(2,1)S(1)}, bf16[128,4096]{1,0:T(8,128)(2,1)S(1)}) conditional(s32[]{:T(128)} %convert_element_type.90, (bf16[128,512]{1,0:T(8,128)(2,1)S(1)}, bf16[128,512]{1,0:T(8,128)(2,1)S(1)}, bf16[128,4096]{1,0:T(8,128)(2,1)S(1)}) %tuple.60, ...), branch_computations={%region_1.1_spmd, %region_2.5_spmd} | conditional | flops 1378849536 | bytes 80869808 | solution.py:96
  1260.8 10.3 collective-permute-done
  1271.1 23.8 %conditional.3 = (bf16[32,4096]{1,0:T(8,128)(2,1)S(1)}, bf16[128,512]{1,0:T(8,128)(2,1)S(1)}, bf16[128,512]{1,0:T(8,128)(2,1)S(1)}, bf16[128,4096]{1,0:T(8,128)(2,1)S(1)}) conditional(s32[]{:T(128)} %convert_element_type.90, (bf16[128,512]{1,0:T(8,128)(2,1)S(1)}, bf16[128,512]{1,0:T(8,128)(2,1)S(1)}, bf16[128,4096]{1,0:T(8,128)(2,1)S(1)}) %tuple.60, ...), branch_computations={%region_1.1_spmd, %region_2.5_spmd} | conditional | flops 1378849536 | bytes 80869808 | solution.py:96
  1296.2 10.3 collective-permute-done
  1306.5 23.8 %conditional.3 = (bf16[32,4096]{1,0:T(8,128)(2,1)S(1)}, bf16[128,512]{1,0:T(8,128)(2,1)S(1)}, bf16[128,512]{1,0:T(8,128)(2,1)S(1)}, bf16[128,4096]{1,0:T(8,128)(2,1)S(1)}) conditional(s32[]{:T(128)} %convert_element_type.90, (bf16[128,512]{1,0:T(8,128)(2,1)S(1)}, bf16[128,512]{1,0:T(8,128)(2,1)S(1)}, bf16[128,4096]{1,0:T(8,128)(2,1)S(1)}) %tuple.60, ...), branch_computations={%region_1.1_spmd, %region_2.5_spmd} | conditional | flops 1378849536 | bytes 80869808 | solution.py:96
  1331.7 10.9 collective-permute-done
  1342.6 23.8 %conditional.3 = (bf16[32,4096]{1,0:T(8,128)(2,1)S(1)}, bf16[128,512]{1,0:T(8,128)(2,1)S(1)}, bf16[128,512]{1,0:T(8,128)(2,1)S(1)}, bf16[128,4096]{1,0:T(8,128)(2,1)S(1)}) conditional(s32[]{:T(128)} %convert_element_type.90, (bf16[128,512]{1,0:T(8,128)(2,1)S(1)}, bf16[128,512]{1,0:T(8,128)(2,1)S(1)}, bf16[128,4096]{1,0:T(8,128)(2,1)S(1)}) %tuple.60, ...), branch_computations={%region_1.1_spmd, %region_2.5_spmd} | conditional | flops 1378849536 | bytes 80869808 | solution.py:96
  (248 shorter events, 312.4 us)
Async XLA Ops:
  6.5 37.8 %all-gather.7.cloned.1.call-start = ((), (), s32[]{:S(2)}) async-start(), calls=%async_computation.1 | async-start | bytes 4718592 | tf_op jit(solution)/shard_map/all_gather | solution.py:21
  7.3 73.6 %all-gather.5.cloned.1.call-start = ((), (), s32[]{:S(2)}) async-start(), calls=%async_computation | async-start | bytes 4718592 | tf_op jit(solution)/shard_map/all_gather | solution.py:22
  8.0 162.2 %all-gather.9.cloned.1.call-start = ((), (), s32[]{:S(2)}) async-start(), calls=%async_computation.2 | async-start | bytes 18874368 | tf_op jit(solution)/shard_map/all_gather | solution.py:20
  8.7 251.4 %all-gather.11.cloned.1.call-start = ((), (), s32[]{:S(2)}) async-start(), calls=%async_computation.3 | async-start | bytes 18874368 | tf_op jit(solution)/shard_map/all_gather | solution.py:23
  316.3 10.4 collective-permute-start
  326.7 11.0 collective-permute-start
  337.7 12.2 collective-permute-start
  350.0 14.0 %collective-permute-start = (bf16[32,4096]{1,0:T(8,128)(2,1)S(1)}, bf16[32,4096]{1,0:T(8,128)(2,1)S(1)}, u32[]{:S(2)}, u32[]{:S(2)}) collective-permute-start(bf16[32,4096]{1,0:T(8,128)(2,1)S(1)} %get-tuple-element.596), channel_id=1, source_target_pairs={{0,8},{8,16},{16,24},{24,32},{32,40},{40,48},{48,56},{56,64},{64,7... | collective-permute-start | bytes 786440 | tf_op jit(solution)/shard_map/while/body/eval_jaxpr/ppermute | solution.py:15
  364.1 12.6 collective-permute-start
  376.7 11.3 collective-permute-start
  417.5 10.4 collective-permute-start
  427.9 11.1 collective-permute-start
  439.1 12.6 collective-permute-start
  451.8 13.8 %collective-permute-start = (bf16[32,4096]{1,0:T(8,128)(2,1)S(1)}, bf16[32,4096]{1,0:T(8,128)(2,1)S(1)}, u32[]{:S(2)}, u32[]{:S(2)}) collective-permute-start(bf16[32,4096]{1,0:T(8,128)(2,1)S(1)} %get-tuple-element.596), channel_id=1, source_target_pairs={{0,8},{8,16},{16,24},{24,32},{32,40},{40,48},{48,56},{56,64},{64,7... | collective-permute-start | bytes 786440 | tf_op jit(solution)/shard_map/while/body/eval_jaxpr/ppermute | solution.py:15
  465.6 12.4 collective-permute-start
  478.1 11.7 collective-permute-start
  519.3 10.4 collective-permute-start
  529.7 11.1 collective-permute-start
  540.9 12.6 collective-permute-start
  571.4 10.4 collective-permute-start
  581.8 653.9 %collective-permute-start = (bf16[32,4096]{1,0:T(8,128)(2,1)S(1)}, bf16[32,4096]{1,0:T(8,128)(2,1)S(1)}, u32[]{:S(2)}, u32[]{:S(2)}) collective-permute-start(bf16[32,4096]{1,0:T(8,128)(2,1)S(1)} %get-tuple-element.596), channel_id=1, source_target_pairs={{0,8},{8,16},{16,24},{24,32},{32,40},{40,48},{48,56},{56,64},{64,7... | collective-permute-start | bytes 786440 | tf_op jit(solution)/shard_map/while/body/eval_jaxpr/ppermute | solution.py:15
  1259.5 11.6 collective-permute-start
  1294.9 11.6 collective-permute-start
  1330.4 12.2 collective-permute-start
  (25 other events, 439.7 us)
Sparse Core Ops, SparseCore 0:
  9.2 35.0 all-gather.6
  46.2 34.6 all-gather.4
  82.7 87.4 all-gather.8
  172.0 88.1 all-gather.10
where the time goes:
time: 1380 us
  waiting for transfers between devices  1230 us (89%)
  matrix products  82.6 us (6%)
  starting transfers between devices  45.3 us (3%)
    ppermute x35, waiting for transfers between devices, passed_along(): lax.ppermute(value, axis, [(source, source + steps) for source in range(i...  972 us
    all_gather x1, waiting for transfers between devices, on_device(): lax.all_gather(w_out, 'dp', axis=1, tiled=True)  89.9 us
    all_gather x1, waiting for transfers between devices, on_device(): lax.all_gather(w_query, 'dp', axis=1, tiled=True)  89.4 us
    ppermute x35, starting transfers between devices, passed_along(): lax.ppermute(value, axis, [(source, source + steps) for source in range(i...  45.2 us
    all_gather x1, waiting for transfers between devices, on_device(): lax.all_gather(w_value, 'dp', axis=1, tiled=True)  36.5 us
    dot_general x4, matrix products, attend(): jnp.dot(normed, weight_q, preferred_element_type=jnp.float32)  35.9 us
    dot_general x4, matrix products, run(): jnp.dot(attended, weight_o, preferred_element_type=jnp.float32)  35 us
    all_gather x1, waiting for transfers between devices, on_device(): lax.all_gather(w_key, 'dp', axis=1, tiled=True)  35 us
  transfers between devices with their start and end apart: 39, of which 39 were waited for; matrix products, arithmetic and copies ran while one was open for 0% of the time, Pallas kernels for 0%

commit v1 on v0

v1 whole, which is shorter than its diff:
```python
import functools

import jax
import jax.numpy as jnp
from jax import lax
from jax.experimental import pallas as pl
from jax.experimental.pallas import tpu as pltpu
from jax.sharding import PartitionSpec as P

MESH = pl.DeviceIdType.MESH
F32 = jnp.float32
BF16 = jnp.bfloat16

SECTIONS = 32
CHIPS = 4
D = 4096
HDIM = 128
SEQ = 128
GROUP = 4
ROWS = 16
PIECES = SEQ // ROWS
COUNT = 2 * PIECES
Q_W, K_W = 1024, 256
QKV_W = Q_W + 2 * K_W
HALF = D // 2
CHUNKS = 4
CW = HALF // CHUNKS
IN_ROWS, OUT_ROWS = 512, 256


def kernel(
    x_ref, gain_ref, wq_ref, wk_ref, wv_ref, wo_ref, out_ref,
    w_in, w_out, hbuf, stage, own_att, sib_att, keys, values, obuf,
    w_recv, w_send, f_send, h_recv, h_send, a_recv, a_send, o_recv, o_send, local,
):
    s = lax.axis_index("section")
    d = lax.axis_index("dp")
    y, c = d // 2, lax.rem(d, 2)
    other = 1 - c
    sibling = (s, y * 2 + other)

    def peer(step, core):
        return (s, lax.rem(y + step + CHIPS, CHIPS) * 2 + core)

    after = lax.rem(s + 1, SECTIONS)
    before = lax.rem(s + SECTIONS - 1, SECTIONS)

    barrier = pltpu.get_barrier_semaphore()
    greeted = [sibling]
    greeted += [peer(step, core) for step in (1, -1) for core in (0, 1)]
    greeted += [(sec, y * 2 + core) for sec in (after, before) for core in (0, 1)]
    for who in greeted:
        pl.semaphore_signal(barrier, inc=1, device_id=who, device_id_type=MESH)
    pl.semaphore_wait(barrier, len(greeted))

    def held(block, mat, core):
        if mat == 3:
            at = lax.rem(block + 8 - 4 * core, 8)
            return w_out.at[pl.ds(pl.multiple_of(at * OUT_ROWS, OUT_ROWS), OUT_ROWS), :]
        first, width = ((0, Q_W), (Q_W, K_W), (Q_W + K_W, K_W))[mat]
        return w_in.at[
            pl.ds(pl.multiple_of(block * IN_ROWS, IN_ROWS), IN_ROWS), pl.ds(first, width)
        ]

    def shard(mat, core):
        ref = (wq_ref, wk_ref, wv_ref, wo_ref)[mat]
        width = (Q_W, K_W, K_W, HALF)[mat]
        return ref.at[0, :, pl.ds(pl.multiple_of(core * width, width), width)]

    def direct(mat, slot, core, target):
        return pltpu.make_async_remote_copy(
            src_ref=shard(mat, core), dst_ref=held(d, mat, core),
            send_sem=w_send.at[mat, slot], recv_sem=w_recv.at[d, mat],
            device_id=target, device_id_type=MESH,
        )

    def forward(mat, slot, block, step):
        return pltpu.make_async_remote_copy(
            src_ref=held(block, mat, c), dst_ref=held(block, mat, c),
            send_sem=f_send.at[mat, slot], recv_sem=w_recv.at[block, mat],
            device_id=peer(step, c), device_id_type=MESH,
        )

    first_step = 2 * c - 1
    directs = []
    for mat in range(4):
        for slot, (step, core) in enumerate(
            ((first_step, c), (first_step, other), (-first_step, c), (-first_step, other))
        ):
            directs.append(direct(mat, slot, core, peer(step, core)))
        directs.append(direct(mat, 4, other, sibling))
    for copy in directs:
        copy.start()
    for mat in range(4):
        pltpu.make_async_copy(shard(mat, c), held(d, mat, c), w_recv.at[d, mat]).start()

    def chunk_cols(core, j):
        return pl.ds(pl.multiple_of(core * HALF + j * CW, CW), CW)

    @pl.when(s == 0)
    def _():
        def spread(p, carry):
            m = 2 * p + c
            copies = []
            for core in (0, 1):
                for j in range(CHUNKS):
                    src = x_ref.at[pl.ds(pl.multiple_of(p * ROWS, ROWS), ROWS), chunk_cols(core, j)]
                    dst = hbuf.at[m, :, chunk_cols(core, j)]
                    pltpu.make_async_copy(src, dst, h_recv.at[m, j, core]).start()
                    copy = pltpu.make_async_remote_copy(
                        src_ref=src, dst_ref=dst,
                        send_sem=h_send.at[0, j, core], recv_sem=h_recv.at[m, j, core],
                        device_id=sibling, device_id_type=MESH,
                    )
                    copy.start()
                    copies.append(copy)
            for copy in copies:
                copy.wait_send()
            return carry

        lax.fori_loop(0, PIECES, spread, 0)

    keys[...] = jnp.zeros_like(keys)
    values[...] = jnp.zeros_like(values)

    def arrived(ref, sem):
        pltpu.make_async_copy(ref, ref, sem).wait()

    from_up = lax.rem(y + 1, CHIPS) * 2
    from_down = lax.rem(y + CHIPS - 1, CHIPS) * 2 + 1
    forwards = []
    for mat in range(4):
        for slot, (block, step) in enumerate(((from_up, -1), (from_down, 1))):
            arrived(held(block, mat, c), w_recv.at[block, mat])
            copy = forward(mat, slot, block, step)
            copy.start()
            forwards.append(copy)
    rest = [
        d,
        y * 2 + other,
        from_up + 1,
        from_down - 1,
        lax.rem(y + 2, CHIPS) * 2,
        lax.rem(y + 2, CHIPS) * 2 + 1,
    ]
    for mat in range(4):
        for block in rest:
            arrived(held(block, mat, c), w_recv.at[block, mat])

    def to_next(m, j, core):
        return pltpu.make_async_remote_copy(
            src_ref=stage.at[m, :, pl.ds(j * CW, CW)], dst_ref=hbuf.at[m, :, chunk_cols(c, j)],
            send_sem=h_send.at[lax.rem(m, 2), j, core], recv_sem=h_recv.at[m, j, c],
            device_id=(after, y * 2 + core), device_id_type=MESH,
        )

    def to_sibling_att(m):
        return pltpu.make_async_remote_copy(
            src_ref=own_att.at[m], dst_ref=sib_att.at[m],
            send_sem=a_send.at[lax.rem(m, 2)], recv_sem=a_recv.at[m],
            device_id=sibling, device_id_type=MESH,
        )

    def out_rows(p):
        return pl.ds(pl.multiple_of(p * ROWS, ROWS), ROWS)

    def to_sibling_out(m):
        p = m // 2
        return pltpu.make_async_remote_copy(
            src_ref=stage.at[m],
            dst_ref=obuf.at[out_rows(p), pl.ds(pl.multiple_of(c * HALF, HALF), HALF)],
            send_sem=o_send.at[p], recv_sem=o_recv.at[p],
            device_id=sibling, device_id_type=MESH,
        )

    row_in_piece = lax.rem(
        lax.broadcasted_iota(jnp.int32, (GROUP * ROWS, SEQ), 0), jnp.int32(ROWS)
    )
    key_pos = lax.broadcasted_iota(jnp.int32, (GROUP * ROWS, SEQ), 1)

    def microbatch(m, carry):
        p, q = m // 2, lax.rem(m, 2)

        acc = jnp.zeros((ROWS, QKV_W), F32)
        squares = jnp.zeros((ROWS, 1), F32)
        for j in range(CHUNKS):
            for core in (0, 1):
                cols = pl.ds(core * HALF + j * CW, CW)
                arrived(hbuf.at[m, :, cols], h_recv.at[m, j, core])
                x = hbuf[m, :, cols].astype(F32)
                squares = squares + jnp.sum(x * x, axis=-1, keepdims=True)
                scaled = (x * gain_ref[:, cols]).astype(BF16)
                acc = acc + jnp.dot(scaled, w_in[cols, :], preferred_element_type=F32)
        acc = acc * lax.rsqrt(squares * (1.0 / D) + 1e-5)
        acc = acc.astype(BF16)
        rows = out_rows(p)
        keys[q, rows, :] = acc[:, Q_W : Q_W + K_W]
        values[q, rows, :] = acc[:, Q_W + K_W :]

        allowed = key_pos <= row_in_piece + p * ROWS
        for g in range(2):
            query = jnp.concatenate(
                [
                    acc[:, (g * GROUP + h) * HDIM : (g * GROUP + h + 1) * HDIM]
                    for h in range(GROUP)
                ],
                axis=0,
            )
            k = keys[q, :, g * HDIM : (g + 1) * HDIM]
            v = values[q, :, g * HDIM : (g + 1) * HDIM]
            scores = lax.dot_general(
                query, k, (((1,), (1,)), ((), ())), preferred_element_type=F32
            ) * (1.0 / HDIM**0.5)
            scores = jnp.where(allowed, scores, -1e30)
            expo = jnp.exp(scores - jnp.max(scores, axis=-1, keepdims=True))
            probs = (expo / jnp.sum(expo, axis=-1, keepdims=True)).astype(BF16)
            attended = jnp.dot(probs, v, preferred_element_type=F32).astype(BF16)
            for h in range(GROUP):
                at = (g * GROUP + h) * HDIM
                own_att[m, :, at : at + HDIM] = attended[h * ROWS : (h + 1) * ROWS, :]

        @pl.when(m >= 2)
        def _():
            to_sibling_att(m - 2).wait_send()

            @pl.when(s < SECTIONS - 1)
            def _():
                for j in range(CHUNKS):
                    for core in (0, 1):
                        to_next(m - 2, j, core).wait_send()

        to_sibling_att(m).start()

        own = jnp.dot(own_att[m], w_out[:Q_W, :], preferred_element_type=F32)
        arrived(sib_att.at[m], a_recv.at[m])
        sib = sib_att[m]
        for j in range(CHUNKS):
            cols = slice(j * CW, (j + 1) * CW)
            total = own[:, cols] + jnp.dot(sib, w_out[Q_W:, cols], preferred_element_type=F32)
            total = total + hbuf[m, :, chunk_cols(c, j)].astype(F32)
            stage[m, :, cols] = total.astype(BF16)

            @pl.when(s < SECTIONS - 1)
            def _():
                for core in (0, 1):
                    to_next(m, j, core).start()

        @pl.when(q == c)
        def _():
            obuf[rows, pl.ds(pl.multiple_of(c * HALF, HALF), HALF)] = stage[m]

        @pl.when(q != c)
        def _():
            to_sibling_out(m).start()

        return carry

    lax.fori_loop(0, COUNT, microbatch, 0)

    for m in (COUNT - 2, COUNT - 1):
        to_sibling_att(m).wait_send()

        @pl.when(s < SECTIONS - 1)
        def _():
            for j in range(CHUNKS):
                for core in (0, 1):
                    to_next(m, j, core).wait_send()

    def settle(p, carry):
        to_sibling_out(2 * p + other).wait_send()
        ref = obuf.at[out_rows(p), pl.ds(pl.multiple_of(other * HALF, HALF), HALF)]
        arrived(ref, o_recv.at[p])
        return carry

    lax.fori_loop(0, PIECES, settle, 0)
    result = pltpu.make_async_copy(obuf, out_ref.at[0], local)
    result.start()
    for copy in directs + forwards:
        copy.wait_send()
    result.wait()


def on_device(inputs, gains, w_query, w_key, w_value, w_out):
    anywhere = pl.BlockSpec(memory_space=pl.ANY)
    vmem = pl.BlockSpec(memory_space=pltpu.VMEM)
    dma = pltpu.SemaphoreType.DMA
    return pl.pallas_call(
        kernel,
        out_shape=jax.ShapeDtypeStruct((1, SEQ, D), BF16),
        in_specs=[anywhere, vmem, anywhere, anywhere, anywhere, anywhere],
        out_specs=anywhere,
        scratch_shapes=[
            pltpu.VMEM((D, QKV_W), BF16),
            pltpu.VMEM((2 * Q_W, HALF), BF16),
            pltpu.VMEM((COUNT, ROWS, D), BF16),
            pltpu.VMEM((COUNT, ROWS, HALF), BF16),
            pltpu.VMEM((COUNT, ROWS, Q_W), BF16),
            pltpu.VMEM((COUNT, ROWS, Q_W), BF16),
            pltpu.VMEM((2, SEQ, K_W), BF16),
            pltpu.VMEM((2, SEQ, K_W), BF16),
            pltpu.VMEM((SEQ, D), BF16),
            dma((8, 4)),
            dma((4, 5)),
            dma((4, 2)),
            dma((COUNT, CHUNKS, 2)),
            dma((2, CHUNKS, 2)),
            dma((COUNT,)),
            dma((2,)),
            dma((PIECES,)),
            dma((PIECES,)),
            dma(()),
        ],
        compiler_params=pltpu.CompilerParams(
            collective_id=0, has_side_effects=True, vmem_limit_bytes=56 * 2**20
        ),
    )(inputs, gains, w_query, w_key, w_value, w_out)


def solution(mesh):
    in_specs = (
        P("dp", None),
        P("section", None),
        P("section", "dp", None),
        P("section", "dp", None),
        P("section", "dp", None),
        P("section", "dp", None),
    )
    return jax.shard_map(
        on_device,
        mesh=mesh,
        in_specs=in_specs,
        out_specs=P("section", "dp", None),
        check_vma=False,
    )
```

time: 1380 us -> 490 us (0.36)
  waiting for transfers between devices: 1230 us -> 0 us
  Pallas kernels: 0 us -> 487 us
  matrix products: 82.6 us -> 0 us
  starting transfers between devices: 45.3 us -> 0 us
    ppermute x35 -> x0, waiting for transfers between devices: 972 us -> none  [passed_along(): lax.ppermute(value, axis, [(source, source + steps) for source in range(i...]
    pallas_call x0 -> x1, Pallas kernels: none -> 487 us  [on_device(): pl.pallas_call(kernel, out_shape=jax.ShapeDtypeStruct((1, SEQ, D), BF16),...]
    all_gather x4 -> x0, waiting for transfers between devices: 251 us -> none  [the longest x1 89.9 us: on_device(): lax.all_gather(w_out, 'dp', axis=1, tiled=True)]
    dot_general x24 -> x0, matrix products: 82.6 us -> none  [the longest x4 35.9 us: attend(): jnp.dot(normed, weight_q, preferred_element_type=jnp.float32)]
    ppermute x35 -> x0, starting transfers between devices: 45.2 us -> none  [passed_along(): lax.ppermute(value, axis, [(source, source + steps) for source in range(i...]
  transfers between devices with their start and end apart: 39 -> 0, of which waited for: 39 -> 0; matrix products, arithmetic and copies ran while one was open for 0% -> 0% of each run, Pallas kernels for 0% -> 0%
where the time goes in v1:
time: 490 us; the launch traced here: 489 us
  Pallas kernels  487 us (99%)
    pallas_call x1, Pallas kernels, on_device(): pl.pallas_call(kernel, out_shape=jax.ShapeDtypeStruct((1, SEQ, D), BF16),...  487 us

profile of v1, /device:TPU:230, one launch (start us, length us, event | category | flops | bytes accessed | tf_op | source)
XLA Modules:
  0.0 489.0 jit_solution(8575679316328772080)
XLA Ops:
  0.0 486.7 %shard_map.64 = bf16[1,128,4096]{2,1,0:T(8,128)(2,1)} custom-call(bf16[128,4096]{1,0:T(8,128)(2,1)} %x_ref.1, f32[1,4096]{1,0:T(1,128)} %gain_ref.1, bf16[1,512,2048]{2,1,0:T(8,128)(2,1)} %wq_ref.1, bf16[1,512,512]{2,1,0:T(8,128)(2,1)} %wk_ref.1, bf16[1,512,512]{2,1,0:T(8,128)(2,1)} %wv_ref.1, bf16[1,256,4096]{2,1,0:T(8,128)(2,1)} %wo_ref.1), custom_call_target="tpu_custom_call" | custom-call | tf_op jit(solution)/shard_map/pallas_call | solution.py:287
  486.7 2.3 copy.8

commit v2 on v1

v2 whole, which is shorter than its diff:
```python
import functools

import jax
import jax.numpy as jnp
from jax import lax
from jax.experimental import pallas as pl
from jax.experimental.pallas import tpu as pltpu
from jax.sharding import PartitionSpec as P

MESH = pl.DeviceIdType.MESH
F32 = jnp.float32
BF16 = jnp.bfloat16

SECTIONS = 32
CHIPS = 4
D = 4096
HDIM = 128
SEQ = 128
GROUP = 4
G_W = GROUP * HDIM
ROWS = 16
PIECES = SEQ // ROWS
COUNT = 2 * PIECES
Q_W, K_W = 1024, 256
QKV_W = Q_W + 2 * K_W
HALF = D // 2
CHUNKS = 4
CW = HALF // CHUNKS
IN_ROWS, OUT_ROWS = 512, 256
PART = OUT_ROWS // 4
MATS = 3 + OUT_ROWS // PART
XS, ZS = 4, 8
DETOURS = 3


def kernel(
    x_ref, gain_ref, wq_ref, wk_ref, wv_ref, wo_ref, out_ref,
    w_in, w_out, lent, hbuf, stage, own_att, sib_att, keys, values, obuf,
    w_recv, w_send, f_send, l_recv, l_send, ld_send, lf_send, b_send, h_recv, h_send, r_send, a_recv, a_send, o_recv, o_send, local,
):
    s = lax.axis_index("section")
    d = lax.axis_index("dp")
    z, x_pos = s // XS, lax.rem(s, XS)
    y, c = d // 2, lax.rem(d, 2)
    other = 1 - c
    sibling = (s, y * 2 + other)

    def peer(step, core):
        return (s, lax.rem(y + step + CHIPS, CHIPS) * 2 + core)

    after = lax.rem(s + 1, SECTIONS)
    before = lax.rem(s + SECTIONS - 1, SECTIONS)

    barrier = pltpu.get_barrier_semaphore()
    greeted = [sibling]
    greeted += [peer(step, core) for step in (1, -1) for core in (0, 1)]
    above, below = lax.rem(s + XS, SECTIONS), lax.rem(s + SECTIONS - XS, SECTIONS)
    greeted += [(sec, y * 2 + core) for sec in (after, before, above, below) for core in (0, 1)]
    for who in greeted:
        pl.semaphore_signal(barrier, inc=1, device_id=who, device_id_type=MESH)
    pl.semaphore_wait(barrier, len(greeted))

    def part_rows(mat):
        return (mat - 3) * PART

    def held(block, mat, core):
        if not isinstance(mat, int) or mat >= 3:
            at = lax.rem(block + 8 - 4 * core, 8) * OUT_ROWS + part_rows(mat)
            return w_out.at[pl.ds(pl.multiple_of(at, PART), PART), :]
        first, width = ((0, Q_W), (Q_W, K_W), (Q_W + K_W, K_W))[mat]
        return w_in.at[
            pl.ds(pl.multiple_of(block * IN_ROWS, IN_ROWS), IN_ROWS), pl.ds(first, width)
        ]

    def shard(mat, core):
        if mat >= 3:
            cols = pl.ds(pl.multiple_of(core * HALF, HALF), HALF)
            return wo_ref.at[0, pl.ds(part_rows(mat), PART), cols]
        width = (Q_W, K_W, K_W)[mat]
        cols = pl.ds(pl.multiple_of(core * width, width), width)
        return (wq_ref, wk_ref, wv_ref)[mat].at[0, :, cols]

    def direct(mat, slot, core, target):
        return pltpu.make_async_remote_copy(
            src_ref=shard(mat, core), dst_ref=held(d, mat, core),
            send_sem=w_send.at[mat, slot], recv_sem=w_recv.at[d, mat],
            device_id=target, device_id_type=MESH,
        )

    def forward(mat, slot, block, step):
        return pltpu.make_async_remote_copy(
            src_ref=held(block, mat, c), dst_ref=held(block, mat, c),
            send_sem=f_send.at[mat, slot], recv_sem=w_recv.at[block, mat],
            device_id=peer(step, c), device_id_type=MESH,
        )

    def arrived(ref, sem):
        pltpu.make_async_copy(ref, ref, sem).wait()

    def detours(row):
        return jnp.where(row == 0, DETOURS, jnp.where(row < 4, DETOURS - 1, 0))

    mine = detours(z)
    served = jnp.where(z == ZS - 1, 0, z - 1)
    serves = jnp.where(jnp.logical_or(z == ZS - 1, z >= 2), detours(served), 0)
    helper = lax.rem(jnp.where(z == 0, ZS - 1, z + 1), ZS) * XS + x_pos
    client = lax.rem(served + ZS, ZS) * XS + x_pos

    def lend(k, core):
        return pltpu.make_async_remote_copy(
            src_ref=shard(MATS - 1 - k, core), dst_ref=lent.at[k, d],
            send_sem=l_send.at[k, core], recv_sem=l_recv.at[k, d],
            device_id=(helper, y * 2 + core), device_id_type=MESH,
        )

    def lent_on(k, block, sem, step):
        return pltpu.make_async_remote_copy(
            src_ref=lent.at[k, block], dst_ref=lent.at[k, block],
            send_sem=sem, recv_sem=l_recv.at[k, block],
            device_id=peer(step, c), device_id_type=MESH,
        )

    def give_back(k, slot, block):
        mat = MATS - 1 - k
        return pltpu.make_async_remote_copy(
            src_ref=lent.at[k, block], dst_ref=held(block, mat, c),
            send_sem=b_send.at[k, slot], recv_sem=w_recv.at[block, mat],
            device_id=(client, d), device_id_type=MESH,
        )

    from_up = lax.rem(y + 1, CHIPS) * 2
    from_down = lax.rem(y + CHIPS - 1, CHIPS) * 2 + 1
    across = lax.rem(y + 2, CHIPS) * 2
    passed = ((from_up, -1), (from_down, 1))

    def lent_directs(k):
        return [
            lent_on(k, y * 2 + core, ld_send.at[k, core, i], step)
            for core in (0, 1)
            for i, step in enumerate((1, -1))
        ]

    def lent_forwards(k):
        return [
            lent_on(k, block, lf_send.at[k, i], step) for i, (block, step) in enumerate(passed)
        ]

    others = (from_up, from_down, from_up + 1, from_down - 1, across, across + 1)

    def backs(k):
        return [give_back(k, slot, block) for slot, block in enumerate(others)]

    first_step = 2 * c - 1

    def directs(mat):
        return [
            direct(mat, slot, core, peer(step, core))
            for slot, (step, core) in enumerate(
                ((first_step, c), (first_step, other), (-first_step, c), (-first_step, other))
            )
        ]

    def forwards(mat):
        return [forward(mat, slot, block, step) for slot, (block, step) in enumerate(passed)]

    def in_ring(mat):
        return MATS - 1 - mat >= mine

    for k in range(DETOURS):

        @pl.when(k < mine)
        def _(k=k):
            for core in (0, 1):
                lend(k, core).start()

    for mat in range(MATS):
        direct(mat, 4, other, sibling).start()
        pltpu.make_async_copy(shard(mat, c), held(d, mat, c), w_recv.at[d, mat]).start()

    def start_inputs():
        for mat in range(3):
            for copy in directs(mat):
                copy.start()

    @pl.when(z < ZS - 1)
    def _():
        start_inputs()

    def serve(k, carry):
        for core in (0, 1):
            arrived(lent.at[k, y * 2 + core], l_recv.at[k, y * 2 + core])
        for copy in lent_directs(k):
            copy.start()
        onward = lent_forwards(k)
        for slot, block in enumerate(others):
            arrived(lent.at[k, block], l_recv.at[k, block])
            if slot < len(onward):
                onward[slot].start()
            give_back(k, slot, block).start()
        return carry

    lax.fori_loop(0, serves, serve, 0)

    @pl.when(z == ZS - 1)
    def _():
        start_inputs()

    for mat in range(3, MATS):

        @pl.when(in_ring(mat))
        def _(mat=mat):
            for copy in directs(mat):
                copy.start()

    def pass_on(mat):
        for copy, (block, _) in zip(forwards(mat), passed):
            arrived(held(block, mat, c), w_recv.at[block, mat])
            copy.start()

    for mat in range(MATS):
        if mat < 3:
            pass_on(mat)
        else:

            @pl.when(in_ring(mat))
            def _(mat=mat):
                pass_on(mat)

    def chunk_cols(core, j):
        return pl.ds(pl.multiple_of(core * HALF + j * CW, CW), CW)

    @pl.when(s == 0)
    def _():
        def spread(p, carry):
            m = 2 * p + c
            copies = []
            for core in (0, 1):
                for j in range(CHUNKS):
                    src = x_ref.at[pl.ds(pl.multiple_of(p * ROWS, ROWS), ROWS), chunk_cols(core, j)]
                    dst = hbuf.at[m, :, chunk_cols(core, j)]
                    pltpu.make_async_copy(src, dst, h_recv.at[m, j, core]).start()
                    copy = pltpu.make_async_remote_copy(
                        src_ref=src, dst_ref=dst,
                        send_sem=(r_send if core else h_send).at[m, j],
                        recv_sem=h_recv.at[m, j, core],
                        device_id=sibling, device_id_type=MESH,
                    )
                    copy.start()
                    copies.append(copy)
            for copy in copies:
                copy.wait_send()
            return carry

        lax.fori_loop(0, PIECES, spread, 0)

    keys[...] = jnp.zeros_like(keys)
    values[...] = jnp.zeros_like(values)

    for mat in range(MATS):
        for block in (d, y * 2 + other, *others[2:]):
            arrived(held(block, mat, c), w_recv.at[block, mat])
        if mat >= 3:

            @pl.when(jnp.logical_not(in_ring(mat)))
            def _(mat=mat):
                for block in others[:2]:
                    arrived(held(block, mat, c), w_recv.at[block, mat])

    def rows_of(p):
        return pl.ds(pl.multiple_of(p * ROWS, ROWS), ROWS)

    def to_next(m, j):
        return pltpu.make_async_remote_copy(
            src_ref=stage.at[lax.rem(m, 2), rows_of(m // 2), pl.ds(j * CW, CW)],
            dst_ref=hbuf.at[m, :, chunk_cols(c, j)],
            send_sem=h_send.at[m, j], recv_sem=h_recv.at[m, j, c],
            device_id=(after, d), device_id_type=MESH,
        )

    def to_sibling_rows(m, j):
        ref = hbuf.at[m, :, chunk_cols(c, j)]
        return pltpu.make_async_remote_copy(
            src_ref=ref, dst_ref=ref,
            send_sem=r_send.at[m, j], recv_sem=h_recv.at[m, j, c],
            device_id=sibling, device_id_type=MESH,
        )

    def to_sibling_att(m, g):
        return pltpu.make_async_remote_copy(
            src_ref=own_att.at[m, g], dst_ref=sib_att.at[m, g],
            send_sem=a_send.at[m, g], recv_sem=a_recv.at[m, g],
            device_id=sibling, device_id_type=MESH,
        )

    row_in_piece = lax.rem(
        lax.broadcasted_iota(jnp.int32, (GROUP * ROWS, SEQ), 0), jnp.int32(ROWS)
    )
    key_pos = lax.broadcasted_iota(jnp.int32, (GROUP * ROWS, SEQ), 1)

    def microbatch(first, last, m, carry):
        p, q = m // 2, lax.rem(m, 2)
        rows = rows_of(p)

        acc = jnp.zeros((ROWS, QKV_W), F32)
        squares = jnp.zeros((ROWS, 1), F32)
        for core in (c, other):
            for j in range(CHUNKS):
                cols = chunk_cols(core, j)
                arrived(hbuf.at[m, :, cols], h_recv.at[m, j, core])
                if core is c and not first:
                    to_sibling_rows(m, j).start()
                x = hbuf[m, :, cols].astype(F32)
                squares = squares + jnp.sum(x * x, axis=-1, keepdims=True)
                scaled = (x * gain_ref[:, cols]).astype(BF16)
                acc = acc + jnp.dot(scaled, w_in[cols, :], preferred_element_type=F32)
        acc = acc * lax.rsqrt(squares * (1.0 / D) + 1e-5)
        acc = acc.astype(BF16)
        keys[q, rows, :] = acc[:, Q_W : Q_W + K_W]
        values[q, rows, :] = acc[:, Q_W + K_W :]

        allowed = key_pos <= row_in_piece + p * ROWS
        expos = []
        for g in range(2):
            query = jnp.concatenate(
                [
                    acc[:, (g * GROUP + h) * HDIM : (g * GROUP + h + 1) * HDIM]
                    for h in range(GROUP)
                ],
                axis=0,
            )
            scores = lax.dot_general(
                query,
                keys[q, :, g * HDIM : (g + 1) * HDIM],
                (((1,), (1,)), ((), ())),
                preferred_element_type=F32,
            ) * (1.0 / HDIM**0.5)
            scores = jnp.where(allowed, scores, -1e30)
            expos.append(jnp.exp(scores - jnp.max(scores, axis=-1, keepdims=True)))
        sums = [jnp.sum(expo, axis=-1, keepdims=True) for expo in expos]
        for g in range(2):
            attended = jnp.dot(
                expos[g].astype(BF16),
                values[q, :, g * HDIM : (g + 1) * HDIM],
                preferred_element_type=F32,
            )
            attended = (attended / sums[g]).astype(BF16)
            for h in range(GROUP):
                own_att[m, g, :, h * HDIM : (h + 1) * HDIM] = attended[h * ROWS : (h + 1) * ROWS, :]
            to_sibling_att(m, g).start()

        total = hbuf[m, :, pl.ds(pl.multiple_of(c * HALF, HALF), HALF)].astype(F32)
        for g in range(2):
            total = total + jnp.dot(
                own_att[m, g], w_out[g * G_W : (g + 1) * G_W, :], preferred_element_type=F32
            )
        arrived(sib_att.at[m, 0], a_recv.at[m, 0])
        total = total + jnp.dot(
            sib_att[m, 0], w_out[2 * G_W : 3 * G_W, :], preferred_element_type=F32
        )
        arrived(sib_att.at[m, 1], a_recv.at[m, 1])
        sib = sib_att[m, 1]
        for j in range(CHUNKS):
            cols = slice(j * CW, (j + 1) * CW)
            part = total[:, cols] + jnp.dot(
                sib, w_out[3 * G_W :, cols], preferred_element_type=F32
            )
            stage[q, rows, cols] = part.astype(BF16)
            if not last:
                to_next(m, j).start()
        return carry

    def run(first, last):
        lax.fori_loop(0, COUNT, functools.partial(microbatch, first, last), 0)

        def settle(m, carry):
            for g in range(2):
                to_sibling_att(m, g).wait_send()
            for j in range(CHUNKS):
                if not last:
                    to_next(m, j).wait_send()
                if not first:
                    to_sibling_rows(m, j).wait_send()
            return carry

        lax.fori_loop(0, COUNT, settle, 0)

    swap = pltpu.make_async_remote_copy(
        src_ref=stage.at[other], dst_ref=obuf,
        send_sem=o_send, recv_sem=o_recv,
        device_id=sibling, device_id_type=MESH,
    )

    @pl.when(s == 0)
    def _():
        run(True, False)

    @pl.when(jnp.logical_and(s > 0, s < SECTIONS - 1))
    def _():
        run(False, False)

    @pl.when(s == SECTIONS - 1)
    def _():
        run(False, True)

    def result(src, core, sem):
        cols = pl.ds(pl.multiple_of(core * HALF, HALF), HALF)
        return pltpu.make_async_copy(src, out_ref.at[0, :, cols], sem)

    swap.start()
    result(stage.at[c], c, local.at[0]).start()
    swap.wait_recv()
    result(obuf, other, local.at[1]).start()
    for mat in range(MATS):
        direct(mat, 4, other, sibling).wait_send()

        @pl.when(in_ring(mat))
        def _(mat=mat):
            for copy in directs(mat) + forwards(mat):
                copy.wait_send()

    for k in range(DETOURS):

        @pl.when(k < mine)
        def _(k=k):
            for core in (0, 1):
                lend(k, core).wait_send()

    def served_all(k, carry):
        for copy in lent_directs(k) + lent_forwards(k) + backs(k):
            copy.wait_send()
        return carry

    lax.fori_loop(0, serves, served_all, 0)
    swap.wait_send()
    result(stage.at[c], c, local.at[0]).wait()
    result(obuf, other, local.at[1]).wait()


def on_device(inputs, gains, w_query, w_key, w_value, w_out):
    anywhere = pl.BlockSpec(memory_space=pl.ANY)
    vmem = pl.BlockSpec(memory_space=pltpu.VMEM)
    dma = pltpu.SemaphoreType.DMA
    return pl.pallas_call(
        kernel,
        out_shape=jax.ShapeDtypeStruct((1, SEQ, D), BF16),
        in_specs=[anywhere, vmem, anywhere, anywhere, anywhere, anywhere],
        out_specs=anywhere,
        scratch_shapes=[
            pltpu.VMEM((D, QKV_W), BF16),
            pltpu.VMEM((2 * Q_W, HALF), BF16),
            pltpu.VMEM((DETOURS, 8, PART, HALF), BF16),
            pltpu.VMEM((COUNT, ROWS, D), BF16),
            pltpu.VMEM((2, SEQ, HALF), BF16),
            pltpu.VMEM((COUNT, 2, ROWS, G_W), BF16),
            pltpu.VMEM((COUNT, 2, ROWS, G_W), BF16),
            pltpu.VMEM((2, SEQ, K_W), BF16),
            pltpu.VMEM((2, SEQ, K_W), BF16),
            pltpu.VMEM((SEQ, HALF), BF16),
            dma((8, MATS)),
            dma((MATS, 5)),
            dma((MATS, 2)),
            dma((DETOURS, 8)),
            dma((DETOURS, 2)),
            dma((DETOURS, 2, 2)),
            dma((DETOURS, 2)),
            dma((DETOURS, 6)),
            dma((COUNT, CHUNKS, 2)),
            dma((COUNT, CHUNKS)),
            dma((COUNT, CHUNKS)),
            dma((COUNT, 2)),
            dma((COUNT, 2)),
            dma(()),
            dma(()),
            dma((2,)),
        ],
        compiler_params=pltpu.CompilerParams(
            collective_id=0, has_side_effects=True, vmem_limit_bytes=56 * 2**20
        ),
    )(inputs, gains, w_query, w_key, w_value, w_out)


def solution(mesh):
    in_specs = (
        P("dp", None),
        P("section", None),
        P("section", "dp", None),
        P("section", "dp", None),
        P("section", "dp", None),
        P("section", "dp", None),
    )
    return jax.shard_map(
        on_device,
        mesh=mesh,
        in_specs=in_specs,
        out_specs=P("section", "dp", None),
        check_vma=False,
    )
```

time: 490 us -> 420 us (0.86)
  Pallas kernels: 487 us -> 417 us
    pallas_call x1, Pallas kernels: 487 us -> 417 us  [on_device(): pl.pallas_call(kernel, out_shape=jax.ShapeDtypeStruct((1, SEQ, D), BF16),...]
where the time goes in v2:
time: 420 us; the launch traced here: 419 us
  Pallas kernels  417 us (99%)
    pallas_call x1, Pallas kernels, on_device(): pl.pallas_call(kernel, out_shape=jax.ShapeDtypeStruct((1, SEQ, D), BF16),...  417 us

profile of v2, /device:TPU:230, one launch (start us, length us, event | category | flops | bytes accessed | tf_op | source)
XLA Modules:
  0.0 419.0 jit_solution(10785382824176266179)
XLA Ops:
  0.0 416.7 %shard_map.64 = bf16[1,128,4096]{2,1,0:T(8,128)(2,1)} custom-call(bf16[128,4096]{1,0:T(8,128)(2,1)} %x_ref.1, f32[1,4096]{1,0:T(1,128)} %gain_ref.1, bf16[1,512,2048]{2,1,0:T(8,128)(2,1)} %wq_ref.1, bf16[1,512,512]{2,1,0:T(8,128)(2,1)} %wk_ref.1, bf16[1,512,512]{2,1,0:T(8,128)(2,1)} %wv_ref.1, bf16[1,256,4096]{2,1,0:T(8,128)(2,1)} %wo_ref.1), custom_call_target="tpu_custom_call" | custom-call | tf_op jit(solution)/shard_map/pallas_call | solution.py:443
  416.7 2.3 copy.8

commit v3 on v2

--- a/solution.py
+++ b/solution.py
@@ -27,10 +27,12 @@
 CHUNKS = 4
 CW = HALF // CHUNKS
 IN_ROWS, OUT_ROWS = 512, 256
-PART = OUT_ROWS // 4
+PART = OUT_ROWS // 8
 MATS = 3 + OUT_ROWS // PART
 XS, ZS = 4, 8
-DETOURS = 3
+FIRST_OUTER, FIRST_INNER = 5, 2
+LATER = (6, 8, 7, 4)
+DETOURS = max(FIRST_OUTER + FIRST_INNER, *LATER)
 
 
 def kernel(
@@ -97,20 +99,28 @@
     def arrived(ref, sem):
         pltpu.make_async_copy(ref, ref, sem).wait()
 
-    def detours(row):
-        return jnp.where(row == 0, DETOURS, jnp.where(row < 4, DETOURS - 1, 0))
-
-    mine = detours(z)
-    served = jnp.where(z == ZS - 1, 0, z - 1)
-    serves = jnp.where(jnp.logical_or(z == ZS - 1, z >= 2), detours(served), 0)
-    helper = lax.rem(jnp.where(z == 0, ZS - 1, z + 1), ZS) * XS + x_pos
-    client = lax.rem(served + ZS, ZS) * XS + x_pos
+    def by_row(values):
+        total = 0
+        for row, value in values.items():
+            total = total + jnp.where(z == row, value, 0)
+        return total
+
+    mine = by_row({0: FIRST_OUTER + FIRST_INNER, **{r + 1: n for r, n in enumerate(LATER)}})
+    serve_from = by_row({1: FIRST_OUTER})
+    serve_to = by_row(
+        {ZS - 1: FIRST_OUTER, 1: FIRST_OUTER + FIRST_INNER}
+        | {r + 2: n for r, n in enumerate(LATER)}
+    )
+    client = jnp.where(z == ZS - 1, above, below)
+
+    def helper(k):
+        return jnp.where(jnp.logical_and(z == 0, k < FIRST_OUTER), below, above)
 
     def lend(k, core):
         return pltpu.make_async_remote_copy(
             src_ref=shard(MATS - 1 - k, core), dst_ref=lent.at[k, d],
             send_sem=l_send.at[k, core], recv_sem=l_recv.at[k, d],
-            device_id=(helper, y * 2 + core), device_id_type=MESH,
+            device_id=(helper(k), y * 2 + core), device_id_type=MESH,
         )
 
     def lent_on(k, block, sem, step):
@@ -177,14 +187,14 @@
         direct(mat, 4, other, sibling).start()
         pltpu.make_async_copy(shard(mat, c), held(d, mat, c), w_recv.at[d, mat]).start()
 
-    def start_inputs():
-        for mat in range(3):
+    def start_all(mats):
+        for mat in mats:
             for copy in directs(mat):
                 copy.start()
 
     @pl.when(z < ZS - 1)
     def _():
-        start_inputs()
+        start_all((1, 2))
 
     def serve(k, carry):
         for core in (0, 1):
@@ -199,11 +209,13 @@
             give_back(k, slot, block).start()
         return carry
 
-    lax.fori_loop(0, serves, serve, 0)
+    lax.fori_loop(serve_from, serve_to, serve, 0)
 
     @pl.when(z == ZS - 1)
     def _():
-        start_inputs()
+        start_all((1, 2))
+
+    start_all((0,))
 
     for mat in range(3, MATS):
 
@@ -359,14 +371,18 @@
         )
         arrived(sib_att.at[m, 1], a_recv.at[m, 1])
         sib = sib_att[m, 1]
-        for j in range(CHUNKS):
-            cols = slice(j * CW, (j + 1) * CW)
-            part = total[:, cols] + jnp.dot(
-                sib, w_out[3 * G_W :, cols], preferred_element_type=F32
-            )
-            stage[q, rows, cols] = part.astype(BF16)
-            if not last:
-                to_next(m, j).start()
+        parts = []
+        for j in range(CHUNKS + 1):
+            if j < CHUNKS:
+                cols = slice(j * CW, (j + 1) * CW)
+                parts.append(
+                    total[:, cols]
+                    + jnp.dot(sib, w_out[3 * G_W :, cols], preferred_element_type=F32)
+                )
+            if j > 0:
+                stage[q, rows, (j - 1) * CW : j * CW] = parts[j - 1].astype(BF16)
+                if not last:
+                    to_next(m, j - 1).start()
         return carry
 
     def run(first, last):
@@ -430,7 +446,7 @@
             copy.wait_send()
         return carry
 
-    lax.fori_loop(0, serves, served_all, 0)
+    lax.fori_loop(serve_from, serve_to, served_all, 0)
     swap.wait_send()
     result(stage.at[c], c, local.at[0]).wait()
     result(obuf, other, local.at[1]).wait()

time: 420 us -> 409 us (0.974)
  Pallas kernels: 417 us -> 406 us
    pallas_call x1, Pallas kernels: 417 us -> 406 us  [on_device(): pl.pallas_call(kernel, out_shape=jax.ShapeDtypeStruct((1, SEQ, D), BF16),...]
where the time goes in v3:
time: 409 us; the launch traced here: 408 us
  Pallas kernels  406 us (99%)
    pallas_call x1, Pallas kernels, on_device(): pl.pallas_call(kernel, out_shape=jax.ShapeDtypeStruct((1, SEQ, D), BF16),...  406 us

profile of v3, /device:TPU:230, one launch (start us, length us, event | category | flops | bytes accessed | tf_op | source)
XLA Modules:
  0.0 407.8 jit_solution(8269471427924421022)
XLA Ops:
  0.0 405.5 %shard_map.64 = bf16[1,128,4096]{2,1,0:T(8,128)(2,1)} custom-call(bf16[128,4096]{1,0:T(8,128)(2,1)} %x_ref.1, f32[1,4096]{1,0:T(1,128)} %gain_ref.1, bf16[1,512,2048]{2,1,0:T(8,128)(2,1)} %wq_ref.1, bf16[1,512,512]{2,1,0:T(8,128)(2,1)} %wk_ref.1, bf16[1,512,512]{2,1,0:T(8,128)(2,1)} %wv_ref.1, bf16[1,256,4096]{2,1,0:T(8,128)(2,1)} %wo_ref.1), custom_call_target="tpu_custom_call" | custom-call | tf_op jit(solution)/shard_map/pallas_call | solution.py:459
  405.5 2.3 copy.8

commit v4 on v3

--- a/solution.py
+++ b/solution.py
@@ -26,13 +26,29 @@
 HALF = D // 2
 CHUNKS = 4
 CW = HALF // CHUNKS
+EARLY = 2
+DEPTH = 128
 IN_ROWS, OUT_ROWS = 512, 256
 PART = OUT_ROWS // 8
-MATS = 3 + OUT_ROWS // PART
+Q_PARTS = 4
+Q_ROWS = IN_ROWS // Q_PARTS
+OUT_MAT = 2 + Q_PARTS
+MATS = OUT_MAT + OUT_ROWS // PART
 XS, ZS = 4, 8
 FIRST_OUTER, FIRST_INNER = 5, 2
 LATER = (6, 8, 7, 4)
+SERVED_FIRST = 4
 DETOURS = max(FIRST_OUTER + FIRST_INNER, *LATER)
+
+
+def product(rows, weights):
+    total = None
+    for at in range(0, rows.shape[1], DEPTH):
+        term = jnp.dot(
+            rows[:, at : at + DEPTH], weights[at : at + DEPTH, :], preferred_element_type=F32
+        )
+        total = term if total is None else total + term
+    return total
 
 
 def kernel(
@@ -62,25 +78,32 @@
         pl.semaphore_signal(barrier, inc=1, device_id=who, device_id_type=MESH)
     pl.semaphore_wait(barrier, len(greeted))
 
-    def part_rows(mat):
-        return (mat - 3) * PART
+    def out_part(block, mat, core):
+        at = lax.rem(block + 8 - 4 * core, 8) * OUT_ROWS + (mat - OUT_MAT) * PART
+        return w_out.at[pl.ds(pl.multiple_of(at, PART), PART), :]
+
+    def query_part(block, mat):
+        at = pl.multiple_of(block * IN_ROWS + (mat - 2) * Q_ROWS, Q_ROWS)
+        return w_in.at[pl.ds(at, Q_ROWS), pl.ds(0, Q_W)]
 
     def held(block, mat, core):
-        if not isinstance(mat, int) or mat >= 3:
-            at = lax.rem(block + 8 - 4 * core, 8) * OUT_ROWS + part_rows(mat)
-            return w_out.at[pl.ds(pl.multiple_of(at, PART), PART), :]
-        first, width = ((0, Q_W), (Q_W, K_W), (Q_W + K_W, K_W))[mat]
-        return w_in.at[
-            pl.ds(pl.multiple_of(block * IN_ROWS, IN_ROWS), IN_ROWS), pl.ds(first, width)
-        ]
+        if mat < 2:
+            rows = pl.ds(pl.multiple_of(block * IN_ROWS, IN_ROWS), IN_ROWS)
+            return w_in.at[rows, pl.ds(Q_W + mat * K_W, K_W)]
+        return query_part(block, mat) if mat < OUT_MAT else out_part(block, mat, core)
+
+    def query_shard(mat, core):
+        rows = pl.ds(pl.multiple_of((mat - 2) * Q_ROWS, Q_ROWS), Q_ROWS)
+        return wq_ref.at[0, rows, pl.ds(pl.multiple_of(core * Q_W, Q_W), Q_W)]
 
     def shard(mat, core):
-        if mat >= 3:
-            cols = pl.ds(pl.multiple_of(core * HALF, HALF), HALF)
-            return wo_ref.at[0, pl.ds(part_rows(mat), PART), cols]
-        width = (Q_W, K_W, K_W)[mat]
-        cols = pl.ds(pl.multiple_of(core * width, width), width)
-        return (wq_ref, wk_ref, wv_ref)[mat].at[0, :, cols]
+        if mat < 2:
+            cols = pl.ds(pl.multiple_of(core * K_W, K_W), K_W)
+            return (wk_ref, wv_ref)[mat].at[0, :, cols]
+        if mat < OUT_MAT:
+            return query_shard(mat, core)
+        cols = pl.ds(pl.multiple_of(core * HALF, HALF), HALF)
+        return wo_ref.at[0, pl.ds((mat - OUT_MAT) * PART, PART), cols]
 
     def direct(mat, slot, core, target):
         return pltpu.make_async_remote_copy(
@@ -133,7 +156,7 @@
     def give_back(k, slot, block):
         mat = MATS - 1 - k
         return pltpu.make_async_remote_copy(
-            src_ref=lent.at[k, block], dst_ref=held(block, mat, c),
+            src_ref=lent.at[k, block], dst_ref=out_part(block, mat, c),
             send_sem=b_send.at[k, slot], recv_sem=w_recv.at[block, mat],
             device_id=(client, d), device_id_type=MESH,
         )
@@ -162,12 +185,21 @@
 
     first_step = 2 * c - 1
 
+    ways = ((first_step, c), (first_step, other), (-first_step, c), (-first_step, other))
+
     def directs(mat):
         return [
-            direct(mat, slot, core, peer(step, core))
-            for slot, (step, core) in enumerate(
-                ((first_step, c), (first_step, other), (-first_step, c), (-first_step, other))
+            direct(mat, slot, core, peer(step, core)) for slot, (step, core) in enumerate(ways)
+        ]
+
+    def query_directs(mat):
+        return [
+            pltpu.make_async_remote_copy(
+                src_ref=query_shard(mat, core), dst_ref=query_part(d, mat),
+                send_sem=w_send.at[mat, slot], recv_sem=w_recv.at[d, mat],
+                device_id=peer(step, core), device_id_type=MESH,
             )
+            for slot, (step, core) in enumerate(ways)
         ]
 
     def forwards(mat):
@@ -183,24 +215,25 @@
             for core in (0, 1):
                 lend(k, core).start()
 
-    for mat in range(MATS):
-        direct(mat, 4, other, sibling).start()
-        pltpu.make_async_copy(shard(mat, c), held(d, mat, c), w_recv.at[d, mat]).start()
-
-    def start_all(mats):
-        for mat in mats:
-            for copy in directs(mat):
-                copy.start()
+    def start_all(copies):
+        for copy in copies:
+            copy.start()
 
     @pl.when(z < ZS - 1)
     def _():
-        start_all((1, 2))
+        start_all(directs(0) + directs(1))
 
     def serve(k, carry):
         for core in (0, 1):
             arrived(lent.at[k, y * 2 + core], l_recv.at[k, y * 2 + core])
-        for copy in lent_directs(k):
-            copy.start()
+        start_all(lent_directs(k))
+
+        turn = k - serve_from - SERVED_FIRST
+
+        @pl.when(jnp.logical_and(turn >= 0, turn < Q_PARTS))
+        def _():
+            start_all(query_directs(2 + turn))
+
         onward = lent_forwards(k)
         for slot, block in enumerate(others):
             arrived(lent.at[k, block], l_recv.at[k, block])
@@ -213,16 +246,23 @@
 
     @pl.when(z == ZS - 1)
     def _():
-        start_all((1, 2))
-
-    start_all((0,))
-
-    for mat in range(3, MATS):
+        start_all(directs(0) + directs(1))
+
+    for mat in range(2, OUT_MAT):
+
+        @pl.when(mat - 2 >= serve_to - serve_from - SERVED_FIRST)
+        def _(mat=mat):
+            start_all(query_directs(mat))
+
+    for mat in range(OUT_MAT, MATS):
 
         @pl.when(in_ring(mat))
         def _(mat=mat):
-            for copy in directs(mat):
-                copy.start()
+            start_all(directs(mat))
+
+    for mat in range(MATS):
+        direct(mat, 4, other, sibling).start()
+        pltpu.make_async_copy(shard(mat, c), held(d, mat, c), w_recv.at[d, mat]).start()
 
     def pass_on(mat):
         for copy, (block, _) in zip(forwards(mat), passed):
@@ -230,7 +270,7 @@
             copy.start()
 
     for mat in range(MATS):
-        if mat < 3:
+        if mat < OUT_MAT:
             pass_on(mat)
         else:
 
@@ -271,7 +311,7 @@
     for mat in range(MATS):
         for block in (d, y * 2 + other, *others[2:]):
             arrived(held(block, mat, c), w_recv.at[block, mat])
-        if mat >= 3:
+        if mat >= OUT_MAT:
 
             @pl.when(jnp.logical_not(in_ring(mat)))
             def _(mat=mat):
@@ -314,7 +354,7 @@
         rows = rows_of(p)
 
         acc = jnp.zeros((ROWS, QKV_W), F32)
-        squares = jnp.zeros((ROWS, 1), F32)
+        squares = jnp.zeros((ROWS, HDIM), F32)
         for core in (c, other):
             for j in range(CHUNKS):
                 cols = chunk_cols(core, j)
@@ -322,10 +362,13 @@
                 if core is c and not first:
                     to_sibling_rows(m, j).start()
                 x = hbuf[m, :, cols].astype(F32)
-                squares = squares + jnp.sum(x * x, axis=-1, keepdims=True)
+                for at in range(0, CW, HDIM):
+                    part = x[:, at : at + HDIM]
+                    squares = squares + part * part
                 scaled = (x * gain_ref[:, cols]).astype(BF16)
-                acc = acc + jnp.dot(scaled, w_in[cols, :], preferred_element_type=F32)
-        acc = acc * lax.rsqrt(squares * (1.0 / D) + 1e-5)
+                acc = acc + product(scaled, w_in[cols, :])
+        mean = jnp.sum(squares, axis=-1, keepdims=True) * (1.0 / D)
+        acc = acc * lax.rsqrt(mean + 1e-5)
         acc = acc.astype(BF16)
         keys[q, rows, :] = acc[:, Q_W : Q_W + K_W]
         values[q, rows, :] = acc[:, Q_W + K_W :]
@@ -348,37 +391,41 @@
             ) * (1.0 / HDIM**0.5)
             scores = jnp.where(allowed, scores, -1e30)
             expos.append(jnp.exp(scores - jnp.max(scores, axis=-1, keepdims=True)))
-        sums = [jnp.sum(expo, axis=-1, keepdims=True) for expo in expos]
+        factors = [1.0 / jnp.sum(expo, axis=-1, keepdims=True) for expo in expos]
+        owns = []
         for g in range(2):
             attended = jnp.dot(
                 expos[g].astype(BF16),
                 values[q, :, g * HDIM : (g + 1) * HDIM],
                 preferred_element_type=F32,
             )
-            attended = (attended / sums[g]).astype(BF16)
-            for h in range(GROUP):
-                own_att[m, g, :, h * HDIM : (h + 1) * HDIM] = attended[h * ROWS : (h + 1) * ROWS, :]
+            attended = (attended * factors[g]).astype(BF16)
+            attended = jnp.concatenate(
+                [attended[h * ROWS : (h + 1) * ROWS, :] for h in range(GROUP)], axis=1
+            )
+            own_att[m, g] = attended
+            owns.append(attended)
             to_sibling_att(m, g).start()
 
         total = hbuf[m, :, pl.ds(pl.multiple_of(c * HALF, HALF), HALF)].astype(F32)
         for g in range(2):
-            total = total + jnp.dot(
-                own_att[m, g], w_out[g * G_W : (g + 1) * G_W, :], preferred_element_type=F32
-            )
+            total = total + product(owns[g], w_out[g * G_W : (g + 1) * G_W, :])
+
+        def third(j):
+            cols = slice(j * CW, (j + 1) * CW)
+            return total[:, cols] + product(sib_0, w_out[2 * G_W : 3 * G_W, cols])
+
         arrived(sib_att.at[m, 0], a_recv.at[m, 0])
-        total = total + jnp.dot(
-            sib_att[m, 0], w_out[2 * G_W : 3 * G_W, :], preferred_element_type=F32
-        )
+        sib_0 = sib_att[m, 0]
+        parts = [third(j) for j in range(EARLY)]
         arrived(sib_att.at[m, 1], a_recv.at[m, 1])
-        sib = sib_att[m, 1]
-        parts = []
+        sib_1 = sib_att[m, 1]
         for j in range(CHUNKS + 1):
             if j < CHUNKS:
+                if j >= EARLY:
+                    parts.append(third(j))
                 cols = slice(j * CW, (j + 1) * CW)
-                parts.append(
-                    total[:, cols]
-                    + jnp.dot(sib, w_out[3 * G_W :, cols], preferred_element_type=F32)
-                )
+                parts[j] = parts[j] + product(sib_1, w_out[3 * G_W :, cols])
             if j > 0:
                 stage[q, rows, (j - 1) * CW : j * CW] = parts[j - 1].astype(BF16)
                 if not last:

time: 409 us -> 396 us (0.968)
  Pallas kernels: 406 us -> 393 us
    pallas_call x1, Pallas kernels: 406 us -> 393 us  [on_device(): pl.pallas_call(kernel, out_shape=jax.ShapeDtypeStruct((1, SEQ, D), BF16),...]
where the time goes in v4:
time: 396 us; the launch traced here: 395 us
  Pallas kernels  393 us (99%)
    pallas_call x1, Pallas kernels, on_device(): pl.pallas_call(kernel, out_shape=jax.ShapeDtypeStruct((1, SEQ, D), BF16),...  393 us

profile of v4, /device:TPU:230, one launch (start us, length us, event | category | flops | bytes accessed | tf_op | source)
XLA Modules:
  0.0 395.3 jit_solution(3027667097832051769)
XLA Ops:
  0.0 393.0 %shard_map.64 = bf16[1,128,4096]{2,1,0:T(8,128)(2,1)} custom-call(bf16[128,4096]{1,0:T(8,128)(2,1)} %x_ref.1, f32[1,4096]{1,0:T(1,128)} %gain_ref.1, bf16[1,512,2048]{2,1,0:T(8,128)(2,1)} %wq_ref.1, bf16[1,512,512]{2,1,0:T(8,128)(2,1)} %wk_ref.1, bf16[1,512,512]{2,1,0:T(8,128)(2,1)} %wv_ref.1, bf16[1,256,4096]{2,1,0:T(8,128)(2,1)} %wo_ref.1), custom_call_target="tpu_custom_call" | custom-call | tf_op jit(solution)/shard_map/pallas_call | solution.py:506
  393.0 2.3 copy.8

commit v5 on v4

--- a/solution.py
+++ b/solution.py
@@ -281,29 +281,28 @@
     def chunk_cols(core, j):
         return pl.ds(pl.multiple_of(core * HALF + j * CW, CW), CW)
 
+    def spread(p, core, j, remote):
+        m = 2 * p + c
+        src = x_ref.at[pl.ds(pl.multiple_of(p * ROWS, ROWS), ROWS), chunk_cols(core, j)]
+        dst = hbuf.at[m, :, chunk_cols(core, j)]
+        if not remote:
+            return pltpu.make_async_copy(src, dst, h_recv.at[m, j, core])
+        return pltpu.make_async_remote_copy(
+            src_ref=src, dst_ref=dst,
+            send_sem=r_send.at[2 * p + core, j], recv_sem=h_recv.at[m, j, core],
+            device_id=sibling, device_id_type=MESH,
+        )
+
     @pl.when(s == 0)
     def _():
-        def spread(p, carry):
-            m = 2 * p + c
-            copies = []
+        def start_piece(p, carry):
             for core in (0, 1):
                 for j in range(CHUNKS):
-                    src = x_ref.at[pl.ds(pl.multiple_of(p * ROWS, ROWS), ROWS), chunk_cols(core, j)]
-                    dst = hbuf.at[m, :, chunk_cols(core, j)]
-                    pltpu.make_async_copy(src, dst, h_recv.at[m, j, core]).start()
-                    copy = pltpu.make_async_remote_copy(
-                        src_ref=src, dst_ref=dst,
-                        send_sem=(r_send if core else h_send).at[m, j],
-                        recv_sem=h_recv.at[m, j, core],
-                        device_id=sibling, device_id_type=MESH,
-                    )
-                    copy.start()
-                    copies.append(copy)
-            for copy in copies:
-                copy.wait_send()
+                    for remote in (False, True):
+                        spread(p, core, j, remote).start()
             return carry
 
-        lax.fori_loop(0, PIECES, spread, 0)
+        lax.fori_loop(0, PIECES, start_piece, 0)
 
     keys[...] = jnp.zeros_like(keys)
     values[...] = jnp.zeros_like(values)
@@ -426,26 +425,28 @@
                     parts.append(third(j))
                 cols = slice(j * CW, (j + 1) * CW)
                 parts[j] = parts[j] + product(sib_1, w_out[3 * G_W :, cols])
-            if j > 0:
-                stage[q, rows, (j - 1) * CW : j * CW] = parts[j - 1].astype(BF16)
+            ready = 0 if j == 0 else j - 1
+            if j != 1:
+                stage[q, rows, ready * CW : (ready + 1) * CW] = parts[ready].astype(BF16)
                 if not last:
-                    to_next(m, j - 1).start()
+                    to_next(m, ready).start()
         return carry
 
     def run(first, last):
         lax.fori_loop(0, COUNT, functools.partial(microbatch, first, last), 0)
 
-        def settle(m, carry):
-            for g in range(2):
-                to_sibling_att(m, g).wait_send()
+    def settle(first, last, m, carry):
+        for g in range(2):
+            to_sibling_att(m, g).wait_send()
+        for j in range(CHUNKS):
+            if not last:
+                to_next(m, j).wait_send()
+            if not first:
+                to_sibling_rows(m, j).wait_send()
+        if first:
             for j in range(CHUNKS):
-                if not last:
-                    to_next(m, j).wait_send()
-                if not first:
-                    to_sibling_rows(m, j).wait_send()
-            return carry
-
-        lax.fori_loop(0, COUNT, settle, 0)
+                spread(m // 2, lax.rem(m, 2), j, True).wait_send()
+        return carry
 
     swap = pltpu.make_async_remote_copy(
         src_ref=stage.at[other], dst_ref=obuf,
@@ -473,6 +474,19 @@
     result(stage.at[c], c, local.at[0]).start()
     swap.wait_recv()
     result(obuf, other, local.at[1]).start()
+
+    @pl.when(s == 0)
+    def _():
+        lax.fori_loop(0, COUNT, functools.partial(settle, True, False), 0)
+
+    @pl.when(jnp.logical_and(s > 0, s < SECTIONS - 1))
+    def _():
+        lax.fori_loop(0, COUNT, functools.partial(settle, False, False), 0)
+
+    @pl.when(s == SECTIONS - 1)
+    def _():
+        lax.fori_loop(0, COUNT, functools.partial(settle, False, True), 0)
+
     for mat in range(MATS):
         direct(mat, 4, other, sibling).wait_send()
 

time: 396 us -> 397 us (level)
  no operation moved by 1% of the time
where the time goes in v5:
time: 397 us; the launch traced here: 396 us
  Pallas kernels  394 us (99%)
    pallas_call x1, Pallas kernels, on_device(): pl.pallas_call(kernel, out_shape=jax.ShapeDtypeStruct((1, SEQ, D), BF16),...  394 us

profile of v5, /device:TPU:230, one launch (start us, length us, event | category | flops | bytes accessed | tf_op | source)
XLA Modules:
  0.0 396.5 jit_solution(7163176817895744534)
XLA Ops:
  0.0 394.2 %shard_map.64 = bf16[1,128,4096]{2,1,0:T(8,128)(2,1)} custom-call(bf16[128,4096]{1,0:T(8,128)(2,1)} %x_ref.1, f32[1,4096]{1,0:T(1,128)} %gain_ref.1, bf16[1,512,2048]{2,1,0:T(8,128)(2,1)} %wq_ref.1, bf16[1,512,512]{2,1,0:T(8,128)(2,1)} %wk_ref.1, bf16[1,512,512]{2,1,0:T(8,128)(2,1)} %wv_ref.1, bf16[1,256,4096]{2,1,0:T(8,128)(2,1)} %wo_ref.1), custom_call_target="tpu_custom_call" | custom-call | tf_op jit(solution)/shard_map/pallas_call | solution.py:520
  394.2 2.3 copy.8
